TPU v7x, 128 devices: a whole 4x4x4 slice. The times are simulated.
128 devices in a mesh: grp: 4 (over z), ep: 32 (over x, y, core).
Axes of the slice: x: 4, y: 4, z: 4, core: 2. Of those that a mesh axis runs over, the one named last changes fastest.
Arguments:
- attention: bfloat16 [16384, 1024], P(('grp', 'ep')), may hold values from -6 to 6
- residual: bfloat16 [16384, 1024], P(('grp', 'ep')), may hold values from -6 to 6
- out_proj: bfloat16 [1024, 1024], P(None, 'grp'), may hold values from -0.1875 to 0.1875
- pre_gain: float32 [1024], replicated, may hold values from 0.25 to 1.75
- post_gain: float32 [1024], replicated, may hold values from 0.25 to 1.75
- slot_gate_up: bfloat16 [32, 1024, 1024], P('ep'), may hold values from -0.1875 to 0.1875
- slot_down: bfloat16 [32, 512, 1024], P('ep'), may hold values from -0.25 to 0.25
- expert_ids: int32 [16384, 8], P(('grp', 'ep')), may hold values from 0 to 31, all different within a row
- copy_choice: int32 [16384, 8], P(('grp', 'ep')), may hold values from 0 to 3
- placement: int32 [32], replicated, may hold values from 0 to 31, each once
- request_age: int32 [16384], P(('grp', 'ep')), may hold values from 0 to 1048575
- decode_flag: int32 [16384], P(('grp', 'ep')), may hold values 0 or 1
- capacity: int32 [4, 32], replicated, may hold values from 4 to 8, as said below
- route_weight: float32 [16384, 8], P(('grp', 'ep')), may hold values from 0.05 to 1
Outputs:
- layer_out: bfloat16 [16384, 1024], P(('grp', 'ep'))
Inputs may be any that keep to these rules, and one draw needn't show every extreme that they name: At least one block has capacity 8. `expert_ids`: each row names 8 different experts. `placement`: each slot holds a different expert.
All inputs are finite; a program needn't handle non-finite values. No bound on the sum of `decode_flag` on one device may be relied on, other than what follows from the above.
Results may differ from a plain program's by a relative error of at most 0.01.
Values may be sent and summed in bfloat16 or wider, within the bound.
A program may use at most 64 MiB of HBM per device.

v0:
```python
import jax
import jax.numpy as jnp
from jax import lax
from jax.sharding import PartitionSpec as P


def rms_scale(values, gain):
    meansq = jnp.mean(values * values, axis=-1, keepdims=True)
    return values * lax.rsqrt(meansq + 1e-06) * gain


def on_device(
    attention,
    residual,
    out_proj,
    pre_gain,
    post_gain,
    slot_gate_up,
    slot_down,
    expert_ids,
    copy_choice,
    placement,
    request_age,
    decode_flag,
    capacity,
    route_weight,
):
    groups = lax.axis_size("grp")
    owners = lax.axis_size("ep")
    devices_all = groups * owners
    rows_here = attention.shape[0]
    features = attention.shape[1]
    picks_row = expert_ids.shape[1]
    cap_size = max(2, rows_here * picks_row // devices_all)
    columns = jnp.dot(
        lax.all_gather(attention, "grp", axis=0, tiled=True),
        out_proj,
        preferred_element_type=jnp.float32,
    )
    attn_proj = lax.all_to_all(columns, "grp", split_axis=0, concat_axis=1, tiled=True)
    hidden_state = (residual.astype(jnp.float32) + attn_proj).astype(jnp.bfloat16)
    normed = rms_scale(hidden_state.astype(jnp.float32), pre_gain).astype(jnp.bfloat16)
    experts_all = placement.shape[0]
    slot_table = jnp.arange(owners, dtype=jnp.int32)
    matches = (placement[None, :] == jnp.arange(experts_all, dtype=jnp.int32)[:, None]).astype(
        jnp.int32
    )
    slot_of = jnp.sum(slot_table[None, :] * matches, axis=1)
    expert_hits = (
        expert_ids[:, :, None] == jnp.arange(experts_all, dtype=jnp.int32)[None, None, :]
    ).astype(jnp.int32)
    target = copy_choice * owners + jnp.sum(expert_hits * slot_of[None, None, :], axis=2)
    priority = decode_flag * 1048576 + request_age
    order = jnp.arange(rows_here, dtype=jnp.int32)
    ahead_mask = (priority[None, :] > priority[:, None]) | (
        priority[None, :] == priority[:, None]
    ) & (order[None, :] < order[:, None])
    target_hits = jnp.sum(
        (target[:, :, None] == jnp.arange(devices_all, dtype=jnp.int32)[None, None, :]).astype(
            jnp.bfloat16
        ),
        axis=1,
    )
    counts = jnp.dot(
        ahead_mask.astype(jnp.bfloat16), target_hits, preferred_element_type=jnp.float32
    )
    position = jnp.take_along_axis(counts, target, axis=1).astype(jnp.int32)
    granted = jnp.take(capacity.reshape(-1), target)
    accepted = position < granted
    total_slots = devices_all * cap_size
    index = jnp.where(accepted, target * cap_size + position, total_slots)
    spread_rows = jnp.broadcast_to(normed[:, None, :], (rows_here, picks_row, features)).reshape(
        rows_here * picks_row, features
    )
    buffer = (
        jnp.zeros((total_slots, features), jnp.bfloat16)
        .at[index.reshape(-1)]
        .set(spread_rows, mode="drop")
    )
    gate_up_local = slot_gate_up[0]
    down_local = slot_down[0]
    hidden_units = down_local.shape[0]
    arrived = lax.all_to_all(
        buffer.reshape(devices_all, cap_size, features),
        ("grp", "ep"),
        split_axis=0,
        concat_axis=0,
        tiled=True,
    )
    flattened = arrived.reshape(-1, features)
    gate_up = jnp.dot(flattened, gate_up_local, preferred_element_type=jnp.float32)
    expert_hidden = (jax.nn.silu(gate_up[:, :hidden_units]) * gate_up[:, hidden_units:]).astype(
        jnp.bfloat16
    )
    produced = jnp.dot(expert_hidden, down_local, preferred_element_type=jnp.float32).astype(
        jnp.bfloat16
    )
    returned = lax.all_to_all(
        produced.reshape(arrived.shape), ("grp", "ep"), split_axis=0, concat_axis=0, tiled=True
    )
    flat_back = returned.reshape(total_slots, features)
    expert_out = flat_back[jnp.minimum(index, total_slots - 1)]
    weights_kept = jnp.where(accepted, route_weight, jnp.float32(0.0))
    mixture = jnp.einsum("rk,rkd->rd", weights_kept, expert_out, preferred_element_type=jnp.float32)
    return rms_scale(hidden_state.astype(jnp.float32) + mixture, post_gain).astype(jnp.bfloat16)


def solution(mesh):
    placed = (
        P(("grp", "ep"), None),
        P(("grp", "ep"), None),
        P(None, "grp"),
        P(),
        P(),
        P("ep", None, None),
        P("ep", None, None),
        P(("grp", "ep"), None),
        P(("grp", "ep"), None),
        P(),
        P(("grp", "ep")),
        P(("grp", "ep")),
        P(),
        P(("grp", "ep"), None),
    )
    return jax.shard_map(
        on_device, mesh=mesh, in_specs=placed, out_specs=P(("grp", "ep"), None), check_vma=False
    )
```

profile of v0, /device:TPU:1, one launch (start us, length us, event | category | flops | bytes accessed | tf_op | source)
XLA Modules:
  0.0 155.6 jit_solution(14246727109927637221)
XLA Ops:
  6.5 0.7 all-gather.2.cloned.1.call-update
  7.3 0.8 select_reduce_fusion.1
  8.0 0.8 select_reduce_fusion
  8.8 0.7 bitcast_or_fusion
  9.5 0.1 copy.24
  9.6 0.1 copy.25
  9.8 0.2 fusion.17
  10.1 0.7 multiply_add_fusion.1
  10.7 0.2 fusion.20
  10.9 6.8 %gather_fusion.2 = f32[1024]{0:T(1024)S(1)} fusion(f32[128,128]{1,0:T(8,128)S(1)} %fusion.20, s32[1024]{0:T(1024)S(1)} %reshape.110), kind=kCustom, calls=%fused_computation.2 | custom fusion | bytes 16384 | tf_op jit(solution)/shard_map/jit(take_along_axis)/gather | solution.py:67
  17.9 0.1 copy.27
  18.2 6.6 %gather_fusion = s32[1024]{0:T(1024)S(1)} fusion(s32[128]{0:T(128)S(1)} %reshape.87, s32[1024]{0:T(1024)S(1)} %broadcast_clamp_fusion.1), kind=kCustom, calls=%fused_computation | custom fusion | bytes 12288 | tf_op jit(solution)/shard_map/jit(_take)/gather | solution.py:68
  24.9 10.7 %all-gather.2.cloned.1.call-done = bf16[512,1024]{1,0:T(8,128)(2,1)} async-done(((bf16[128,1024]{1,0:T(8,128)(2,1)}), bf16[512,1024]{1,0:T(8,128)(2,1)}) %all-gather.2.cloned.1.call-update) | async-done | bytes 1048592 | tf_op jit(solution)/shard_map/all_gather | solution.py:36
  35.6 2.5 %fusion.27 = f32[512,256]{1,0:T(8,128)} fusion(bf16[512,1024]{1,0:T(8,128)(2,1)} %all-gather.2.cloned.1.call-done, bf16[1024,256]{1,0:T(8,128)(2,1)S(1)} %copy-done.1), kind=kOutput, calls=%fused_computation.57 | convolution fusion | flops 268435456 | bytes 2097152 | tf_op jit(solution)/shard_map/dot_general | solution.py:35
  38.1 3.6 %all-to-all-start = ((f32[4,128,256]{2,1,0:T(8,128)}), f32[4,128,256]{2,1,0:T(8,128)S(1)}, u32[]{:S(2)}, u32[]{:S(2)}) async-start(f32[4,128,256]{2,1,0:T(8,128)} %bitcast), calls=%async_computation | async-start | bytes 1048576 | tf_op jit(solution)/shard_map/all_to_all | solution.py:40
  41.7 0.1 copy.29
  41.8 0.1 reshape.88
  41.9 7.3 %all-to-all-done = f32[4,128,256]{2,1,0:T(8,128)S(1)} async-done(((f32[4,128,256]{2,1,0:T(8,128)}), f32[4,128,256]{2,1,0:T(8,128)S(1)}, u32[]{:S(2)}, u32[]{:S(2)}) %all-to-all-start) | async-done | bytes 524320 | tf_op jit(solution)/shard_map/all_to_all | solution.py:40
  49.2 0.2 fusion.13
  49.4 0.1 fusion.15
  49.6 6.8 %scatter_custom_fusion = bf16[1024,1024]{1,0:T(8,128)(2,1)} fusion(s32[1024]{0:T(1024)S(1)} %bitcast.43, bf16[128,1024]{1,0:T(8,128)(2,1)S(1)} %fusion.15, bf16[]{:T(256)} %constant.29.clone.1), kind=kCustom, calls=%fused_computation.11 | custom fusion | bytes 2359298 | tf_op jit(solution)/shard_map/scatter | solution.py:78
  56.4 40.3 %all_to_all.29 = bf16[128,8,1024]{2,1,0:T(8,128)(2,1)S(1)} all-to-all(bf16[128,8,1024]{2,1,0:T(8,128)(2,1)} %bitcast.40), channel_id=1, replica_groups=mesh['grp'=4,'ep'=32] {'grp','ep'}, dimensions={0} | all-to-all | bytes 4194304 | tf_op jit(solution)/shard_map/all_to_all | solution.py:83
  96.7 2.4 %fusion.3 = f32[1024,1024]{1,0:T(8,128)S(1)} fusion(bf16[1,1024,1024]{2,1,0:T(8,128)(2,1)S(1)} %copy-done, bf16[128,8,1024]{2,1,0:T(8,128)(2,1)S(1)} %all_to_all.29), kind=kOutput, calls=%fused_computation.8 | convolution fusion | flops 2147483648 | bytes 8388608 | tf_op jit(solution)/shard_map/dot_general | solution.py:91
  99.1 2.6 %convert_bitcast_fusion = bf16[128,8,1024]{2,1,0:T(8,128)(2,1)} fusion(f32[1024,1024]{1,0:T(8,128)S(1)} %fusion.3, bf16[1,512,1024]{2,1,0:T(8,128)(2,1)S(1)} %copy-done.7), kind=kOutput, calls=%fused_computation.13 | convolution fusion | flops 1077936128 | bytes 7340032 | tf_op jit(solution)/shard_map/dot_general | solution.py:95
  101.7 5.5 %all-to-all-start.2 = ((bf16[128,8,1024]{2,1,0:T(8,128)(2,1)}), bf16[128,8,1024]{2,1,0:T(8,128)(2,1)}, u32[]{:S(2)}, u32[]{:S(2)}) async-start(bf16[128,8,1024]{2,1,0:T(8,128)(2,1)} %convert_bitcast_fusion), calls=%async_computation.2 | async-start | bytes 4194304 | tf_op jit(solution)/shard_map/all_to_all | solution.py:98
  107.2 0.1 copy.30
  107.5 0.1 copy.31
  107.6 29.9 %all-to-all-done.2 = bf16[128,8,1024]{2,1,0:T(8,128)(2,1)} async-done(((bf16[128,8,1024]{2,1,0:T(8,128)(2,1)}), bf16[128,8,1024]{2,1,0:T(8,128)(2,1)}, u32[]{:S(2)}, u32[]{:S(2)}) %all-to-all-start.2) | async-done | bytes 2097184 | tf_op jit(solution)/shard_map/all_to_all | solution.py:98
  137.5 7.9 %gather_fusion.1 = bf16[1024,1024]{1,0:T(8,128)(2,1)} fusion(bf16[1024,1024]{1,0:T(8,128)(2,1)} %bitcast.11, s32[1024]{0:T(1024)S(1)} %broadcast_clamp_fusion), kind=kCustom, calls=%fused_computation.1 | custom fusion | bytes 4198400 | tf_op jit(solution)/shard_map/gather | solution.py:102
  145.5 2.3 %fusion.1 = f32[128,1,1024]{2,1,0:T(1,128)S(1)} fusion(bf16[128,8,1]{1,2,0:T(2,128)(2,1)S(1)} %copy.31, bf16[1024,1024]{1,0:T(8,128)(2,1)} %gather_fusion.1), kind=kOutput, calls=%fused_computation.6 | convolution fusion | flops 2097152 | bytes 2623488 | tf_op jit(solution)/shard_map/rk,rkd->rd/dot_general | solution.py:104
  147.8 0.2 multiply_reduce_fusion
  147.9 0.8 multiply_convert_fusion
  (34 shorter events, 0.8 us)
Async XLA Ops:
  6.5 90.2 %copy-start = (bf16[1,1024,1024]{2,1,0:T(8,128)(2,1)S(1)}, bf16[1,1024,1024]{2,1,0:T(8,128)(2,1)}, u32[]{:S(2)}) copy-start(bf16[1,1024,1024]{2,1,0:T(8,128)(2,1)} %param.19) | copy-start | bytes 6291460
  6.5 29.1 %all-gather.2.cloned.1.call-start = ((), (), s32[]{:S(2)}) async-start(), calls=%async_computation.3 | async-start | bytes 1310720 | tf_op jit(solution)/shard_map/all_gather | solution.py:36
  10.9 7.2 %copy-start.6 = (s32[4,32]{1,0:T(4,128)S(1)}, s32[4,32]{1,0:T(4,128)}, u32[]{:S(2)}) copy-start(s32[4,32]{1,0:T(4,128)} %param.26) | copy-start | bytes 1540
  18.2 17.4 %copy-start.1 = (bf16[1024,256]{1,0:T(8,128)(2,1)S(1)}, bf16[1024,256]{1,0:T(8,128)(2,1)}, u32[]{:S(2)}) copy-start(bf16[1024,256]{1,0:T(8,128)(2,1)} %param.16) | copy-start | bytes 1572868
  24.9 24.3 %copy-start.2 = (bf16[128,1024]{1,0:T(8,128)(2,1)S(1)}, bf16[128,1024]{1,0:T(8,128)(2,1)}, u32[]{:S(2)}) copy-start(bf16[128,1024]{1,0:T(8,128)(2,1)} %param.15) | copy-start | bytes 786436
  38.1 11.3 %copy-start.3 = (f32[1024]{0:T(1024)S(1)}, f32[1024]{0:T(1024)}, u32[]{:S(2)}) copy-start(f32[1024]{0:T(1024)} %param.17) | copy-start | bytes 12292
  38.1 11.1 %all-to-all-start = ((f32[4,128,256]{2,1,0:T(8,128)}), f32[4,128,256]{2,1,0:T(8,128)S(1)}, u32[]{:S(2)}, u32[]{:S(2)}) async-start(f32[4,128,256]{2,1,0:T(8,128)} %bitcast), calls=%async_computation | async-start | bytes 1048576 | tf_op jit(solution)/shard_map/all_to_all | solution.py:40
  96.7 2.4 %copy-start.7 = (bf16[1,512,1024]{2,1,0:T(8,128)(2,1)S(1)}, bf16[1,512,1024]{2,1,0:T(8,128)(2,1)}, u32[]{:S(2)}) copy-start(bf16[1,512,1024]{2,1,0:T(8,128)(2,1)} %param.20) | copy-start | bytes 3145732
  101.7 5.7 %copy-start.5 = (f32[128,8]{0,1:T(8,128)S(1)}, f32[128,8]{0,1:T(8,128)}, u32[]{:S(2)}) copy-start(f32[128,8]{0,1:T(8,128)} %param.27) | copy-start | bytes 12292
  101.7 35.9 %all-to-all-start.2 = ((bf16[128,8,1024]{2,1,0:T(8,128)(2,1)}), bf16[128,8,1024]{2,1,0:T(8,128)(2,1)}, u32[]{:S(2)}, u32[]{:S(2)}) async-start(bf16[128,8,1024]{2,1,0:T(8,128)(2,1)} %convert_bitcast_fusion), calls=%async_computation.2 | async-start | bytes 4194304 | tf_op jit(solution)/shard_map/all_to_all | solution.py:98
  145.5 2.5 %copy-start.4 = (f32[1024]{0:T(1024)S(1)}, f32[1024]{0:T(1024)}, u32[]{:S(2)}) copy-start(f32[1024]{0:T(1024)} %param.18) | copy-start | bytes 12292
Sparse Core Ops, SparseCore 0:
  9.0 26.5 all-gather.1
where the time goes:
time: 156 us
  waiting for transfers between devices  48.6 us (31%)
  blocking collectives  40.3 us (26%)
  local copies, waits for them, and re-layouts  29.5 us (19%)
  between operations  13.6 us (9%)
  matrix products  9.91 us (6%)
  starting transfers between devices  9.14 us (6%)
  other arithmetic  4.53 us (3%)
    all_to_all x1, blocking collectives, on_device(): lax.all_to_all(buffer.reshape(devices_all, cap_size, features), ('grp', '...  40.3 us
    all_to_all x1, waiting for transfers between devices, on_device(): lax.all_to_all(produced.reshape(arrived.shape), ('grp', 'ep'), split_axis...  29.9 us
    all_gather x1, waiting for transfers between devices, on_device(): lax.all_gather(attention, 'grp', axis=0, tiled=True)  10.7 us
    gather x1, local copies, waits for them, and re-layouts, on_device(): expert_out = flat_back[jnp.minimum(index, total_slots - 1)]  7.92 us
    all_to_all x1, waiting for transfers between devices, on_device(): lax.all_to_all(columns, 'grp', split_axis=0, concat_axis=1, tiled=True)  7.26 us
    gather x5, local copies, waits for them, and re-layouts, on_device(): position = jnp.take_along_axis(counts, target, axis=1).astype(jnp.int32)  7.12 us
    scatter x1, local copies, waits for them, and re-layouts, on_device(): buffer = jnp.zeros((total_slots, features), jnp.bfloat16).at[index.reshap...  6.83 us
    gather x3, local copies, waits for them, and re-layouts, on_device(): granted = jnp.take(capacity.reshape(-1), target)  6.7 us
  transfers between devices with their start and end apart: 3, of which 3 were waited for; matrix products, arithmetic and copies ran while one was open for 12% of the time, Pallas kernels for 0%

commit v1 on v0

--- a/solution.py
+++ b/solution.py
@@ -2,6 +2,19 @@
 import jax.numpy as jnp
 from jax import lax
 from jax.sharding import PartitionSpec as P
+
+
+def refer_runs_all(arr):
+    built, found_now, local_now = (lax.psum(1, "grp"), lax.axis_index("grp"), arr.shape[0])
+    extra, current_block = (arr, 1)
+    while current_block < built:
+        shelf = []
+        for at in [*range(built)]:
+            shelf.append((at, (at - current_block) % built))
+        extra = jnp.concatenate([extra, lax.ppermute(extra, "grp", shelf)], 0)
+        current_block = 2 * current_block
+    main = jnp.roll(extra, found_now * local_now, 0)
+    return main
 
 
 def rms_scale(values, gain):
@@ -32,11 +45,7 @@
     features = attention.shape[1]
     picks_row = expert_ids.shape[1]
     cap_size = max(2, rows_here * picks_row // devices_all)
-    columns = jnp.dot(
-        lax.all_gather(attention, "grp", axis=0, tiled=True),
-        out_proj,
-        preferred_element_type=jnp.float32,
-    )
+    columns = jnp.dot(refer_runs_all(attention), out_proj, preferred_element_type=jnp.float32)
     attn_proj = lax.all_to_all(columns, "grp", split_axis=0, concat_axis=1, tiled=True)
     hidden_state = (residual.astype(jnp.float32) + attn_proj).astype(jnp.bfloat16)
     normed = rms_scale(hidden_state.astype(jnp.float32), pre_gain).astype(jnp.bfloat16)

time: 156 us -> 142 us (0.910)
  between operations: 13.6 us -> 0.24 us
  waiting for transfers between devices: 48.6 us -> 38.8 us
  starting transfers between devices: 9.14 us -> 15.6 us
  other arithmetic: 4.53 us -> 6.29 us
    all_gather x1 -> x0, waiting for transfers between devices: 10.7 us -> none  [on_device(): lax.all_gather(attention, 'grp', axis=0, tiled=True)]
    ppermute x0 -> x2, starting transfers between devices: none -> 6.52 us  [refer_runs_all(): extra = jnp.concatenate([extra, lax.ppermute(extra, 'grp', shelf)], 0)]
    ppermute x0 -> x2, waiting for transfers between devices: none -> 1.81 us  [refer_runs_all(): extra = jnp.concatenate([extra, lax.ppermute(extra, 'grp', shelf)], 0)]
    concatenate x0 -> x1, other arithmetic: none -> 1.76 us  [refer_runs_all(): extra = jnp.concatenate([extra, lax.ppermute(extra, 'grp', shelf)], 0)]
  transfers between devices with their start and end apart: 3 -> 4, of which waited for: 3 -> 3; matrix products, arithmetic and copies ran while one was open for 12% -> 13% of each run, Pallas kernels for 0% -> 0%
where the time goes in v1:
time: 142 us; the launch traced here: 141 us
  blocking collectives  41.2 us (29%)
  waiting for transfers between devices  38.8 us (27%)
  local copies, waits for them, and re-layouts  30.6 us (22%)
  starting transfers between devices  15.6 us (11%)
  matrix products  8.68 us (6%)
  other arithmetic  6.29 us (4%)
    all_to_all x1, blocking collectives, on_device(): lax.all_to_all(buffer.reshape(devices_all, cap_size, features), ('grp', '...  41.2 us
    all_to_all x1, waiting for transfers between devices, on_device(): lax.all_to_all(produced.reshape(arrived.shape), ('grp', 'ep'), split_axis...  29.9 us
    gather x1, local copies, waits for them, and re-layouts, on_device(): expert_out = flat_back[jnp.minimum(index, total_slots - 1)]  7.92 us
    gather x5, local copies, waits for them, and re-layouts, on_device(): position = jnp.take_along_axis(counts, target, axis=1).astype(jnp.int32)  7.12 us
    all_to_all x1, waiting for transfers between devices, on_device(): lax.all_to_all(columns, 'grp', split_axis=0, concat_axis=1, tiled=True)  7.06 us
    scatter x1, local copies, waits for them, and re-layouts, on_device(): buffer = jnp.zeros((total_slots, features), jnp.bfloat16).at[index.reshap...  6.83 us
    gather x3, local copies, waits for them, and re-layouts, on_device(): granted = jnp.take(capacity.reshape(-1), target)  6.7 us
    ppermute x2, starting transfers between devices, refer_runs_all(): extra = jnp.concatenate([extra, lax.ppermute(extra, 'grp', shelf)], 0)  6.52 us
  transfers between devices with their start and end apart: 4, of which 3 were waited for; matrix products, arithmetic and copies ran while one was open for 13% of the time, Pallas kernels for 0%

profile of v1, /device:TPU:1, one launch (start us, length us, event | category | flops | bytes accessed | tf_op | source)
XLA Modules:
  0.0 141.5 jit_solution(15915962606849869417)
XLA Ops:
  0.0 4.6 %collective-permute-start = (bf16[128,1024]{1,0:T(8,128)(2,1)}, bf16[128,1024]{1,0:T(8,128)(2,1)S(1)}, u32[]{:S(2)}, u32[]{:S(2)}) collective-permute-start(bf16[128,1024]{1,0:T(8,128)(2,1)} %param.14), channel_id=1, source_target_pairs={{0,96},{32,0},{64,32},{96,64},{1,97},{33,1},{65,33},{97,65},{2,98}... | collective-permute-start | bytes 786440 | tf_op jit(solution)/shard_map/ppermute | solution.py:14
  4.6 0.8 select_reduce_fusion.1
  5.4 0.8 select_reduce_fusion
  6.1 0.7 bitcast_or_fusion
  6.9 0.7 multiply_add_fusion.1
  7.6 0.2 fusion.19
  7.9 0.2 fusion.22
  8.1 1.8 %collective-permute-done = bf16[128,1024]{1,0:T(8,128)(2,1)S(1)} collective-permute-done((bf16[128,1024]{1,0:T(8,128)(2,1)}, bf16[128,1024]{1,0:T(8,128)(2,1)S(1)}, u32[]{:S(2)}, u32[]{:S(2)}) %collective-permute-start) | collective-permute-done | bytes 262176 | tf_op jit(solution)/shard_map/ppermute | solution.py:14
  9.9 1.8 %pad_maximum_fusion = bf16[256,1024]{1,0:T(8,128)(2,1)} fusion(bf16[128,1024]{1,0:T(8,128)(2,1)S(1)} %collective-permute-done, bf16[128,1024]{1,0:T(8,128)(2,1)} %param.14), kind=kLoop, calls=%fused_computation.26 | loop fusion | flops 1048576 | bytes 1048576 | tf_op jit(solution)/shard_map/concatenate | solution.py:14
  11.6 1.9 %collective-permute-start.1 = (bf16[256,1024]{1,0:T(8,128)(2,1)}, bf16[256,1024]{1,0:T(8,128)(2,1)S(1)}, u32[]{:S(2)}, u32[]{:S(2)}) collective-permute-start(bf16[256,1024]{1,0:T(8,128)(2,1)} %pad_maximum_fusion), channel_id=1, source_target_pairs={{0,64},{32,96},{64,0},{96,32},{1,65},{33,97},{65,1},{97,33},{2,66}... | collective-permute-start | bytes 1572872 | tf_op jit(solution)/shard_map/ppermute | solution.py:14
  13.8 6.8 %gather_fusion.2 = f32[1024]{0:T(1024)S(1)} fusion(f32[128,128]{1,0:T(8,128)S(1)} %fusion.22, s32[1024]{0:T(1024)S(1)} %reshape.110), kind=kCustom, calls=%fused_computation.2 | custom fusion | bytes 16384 | tf_op jit(solution)/shard_map/jit(take_along_axis)/gather | solution.py:76
  20.7 0.1 copy.27
  21.0 6.6 %gather_fusion = s32[1024]{0:T(1024)S(1)} fusion(s32[128]{0:T(128)S(1)} %reshape.87, s32[1024]{0:T(1024)S(1)} %broadcast_clamp_fusion.1), kind=kCustom, calls=%fused_computation | custom fusion | bytes 12288 | tf_op jit(solution)/shard_map/jit(_take)/gather | solution.py:77
  28.0 0.8 copy-done.2
  28.8 1.2 fusion.13
  30.0 3.6 %all-to-all-start = ((f32[4,128,256]{2,1,0:T(8,128)}), f32[4,128,256]{2,1,0:T(8,128)S(1)}, u32[]{:S(2)}, u32[]{:S(2)}) async-start(f32[4,128,256]{2,1,0:T(8,128)} %bitcast), calls=%async_computation | async-start | bytes 1048576 | tf_op jit(solution)/shard_map/all_to_all | solution.py:49
  33.7 0.1 copy.29
  33.9 7.1 %all-to-all-done = f32[4,128,256]{2,1,0:T(8,128)S(1)} async-done(((f32[4,128,256]{2,1,0:T(8,128)}), f32[4,128,256]{2,1,0:T(8,128)S(1)}, u32[]{:S(2)}, u32[]{:S(2)}) %all-to-all-start) | async-done | bytes 524320 | tf_op jit(solution)/shard_map/all_to_all | solution.py:49
  41.0 0.2 fusion.15
  41.2 0.1 fusion.17
  41.3 6.8 %scatter_custom_fusion = bf16[1024,1024]{1,0:T(8,128)(2,1)} fusion(s32[1024]{0:T(1024)S(1)} %bitcast.42, bf16[128,1024]{1,0:T(8,128)(2,1)S(1)} %fusion.17, bf16[]{:T(256)} %constant.78.clone.1), kind=kCustom, calls=%fused_computation.11 | custom fusion | bytes 2359298 | tf_op jit(solution)/shard_map/scatter | solution.py:87
  48.2 41.2 %all_to_all.29 = bf16[128,8,1024]{2,1,0:T(8,128)(2,1)S(1)} all-to-all(bf16[128,8,1024]{2,1,0:T(8,128)(2,1)} %bitcast.39), channel_id=1, replica_groups=mesh['grp'=4,'ep'=32] {'grp','ep'}, dimensions={0} | all-to-all | bytes 4194304 | tf_op jit(solution)/shard_map/all_to_all | solution.py:92
  89.4 2.4 %fusion.3 = f32[1024,1024]{1,0:T(8,128)S(1)} fusion(bf16[1,1024,1024]{2,1,0:T(8,128)(2,1)S(1)} %copy-done, bf16[128,8,1024]{2,1,0:T(8,128)(2,1)S(1)} %all_to_all.29), kind=kOutput, calls=%fused_computation.8 | convolution fusion | flops 2147483648 | bytes 8388608 | tf_op jit(solution)/shard_map/dot_general | solution.py:100
  91.8 2.6 %convert_bitcast_fusion = bf16[128,8,1024]{2,1,0:T(8,128)(2,1)} fusion(f32[1024,1024]{1,0:T(8,128)S(1)} %fusion.3, bf16[1,512,1024]{2,1,0:T(8,128)(2,1)S(1)} %copy-done.8), kind=kOutput, calls=%fused_computation.13 | convolution fusion | flops 1077936128 | bytes 7340032 | tf_op jit(solution)/shard_map/dot_general | solution.py:104
  94.4 5.5 %all-to-all-start.2 = ((bf16[128,8,1024]{2,1,0:T(8,128)(2,1)}), bf16[128,8,1024]{2,1,0:T(8,128)(2,1)}, u32[]{:S(2)}, u32[]{:S(2)}) async-start(bf16[128,8,1024]{2,1,0:T(8,128)(2,1)} %convert_bitcast_fusion), calls=%async_computation.2 | async-start | bytes 4194304 | tf_op jit(solution)/shard_map/all_to_all | solution.py:107
  99.9 0.1 copy.30
  100.1 0.1 copy.31
  100.3 29.9 %all-to-all-done.2 = bf16[128,8,1024]{2,1,0:T(8,128)(2,1)} async-done(((bf16[128,8,1024]{2,1,0:T(8,128)(2,1)}), bf16[128,8,1024]{2,1,0:T(8,128)(2,1)}, u32[]{:S(2)}, u32[]{:S(2)}) %all-to-all-start.2) | async-done | bytes 2097184 | tf_op jit(solution)/shard_map/all_to_all | solution.py:107
  130.2 7.9 %gather_fusion.1 = bf16[1024,1024]{1,0:T(8,128)(2,1)} fusion(bf16[1024,1024]{1,0:T(8,128)(2,1)} %bitcast.11, s32[1024]{0:T(1024)S(1)} %broadcast_clamp_fusion), kind=kCustom, calls=%fused_computation.1 | custom fusion | bytes 4198400 | tf_op jit(solution)/shard_map/gather | solution.py:111
  138.2 2.3 %fusion.1 = f32[128,1,1024]{2,1,0:T(1,128)S(1)} fusion(bf16[128,8,1]{1,2,0:T(2,128)(2,1)S(1)} %copy.31, bf16[1024,1024]{1,0:T(8,128)(2,1)} %gather_fusion.1), kind=kOutput, calls=%fused_computation.6 | convolution fusion | flops 2097152 | bytes 2623488 | tf_op jit(solution)/shard_map/rk,rkd->rd/dot_general | solution.py:113
  140.4 0.2 multiply_reduce_fusion
  140.6 0.8 multiply_convert_fusion
  (44 shorter events, 1.2 us)
Async XLA Ops:
  0.0 89.4 %copy-start = (bf16[1,1024,1024]{2,1,0:T(8,128)(2,1)S(1)}, bf16[1,1024,1024]{2,1,0:T(8,128)(2,1)}, u32[]{:S(2)}) copy-start(bf16[1,1024,1024]{2,1,0:T(8,128)(2,1)} %param.19) | copy-start | bytes 6291460
  0.0 9.9 %collective-permute-start = (bf16[128,1024]{1,0:T(8,128)(2,1)}, bf16[128,1024]{1,0:T(8,128)(2,1)S(1)}, u32[]{:S(2)}, u32[]{:S(2)}) collective-permute-start(bf16[128,1024]{1,0:T(8,128)(2,1)} %param.14), channel_id=1, source_target_pairs={{0,96},{32,0},{64,32},{96,64},{1,97},{33,1},{65,33},{97,65},{2,98}... | collective-permute-start | bytes 786440 | tf_op jit(solution)/shard_map/ppermute | solution.py:14
  11.6 16.2 %collective-permute-start.1 = (bf16[256,1024]{1,0:T(8,128)(2,1)}, bf16[256,1024]{1,0:T(8,128)(2,1)S(1)}, u32[]{:S(2)}, u32[]{:S(2)}) collective-permute-start(bf16[256,1024]{1,0:T(8,128)(2,1)} %pad_maximum_fusion), channel_id=1, source_target_pairs={{0,64},{32,96},{64,0},{96,32},{1,65},{33,97},{65,1},{97,33},{2,66}... | collective-permute-start | bytes 1572872 | tf_op jit(solution)/shard_map/ppermute | solution.py:14
  13.8 7.2 %copy-start.7 = (s32[4,32]{1,0:T(4,128)S(1)}, s32[4,32]{1,0:T(4,128)}, u32[]{:S(2)}) copy-start(s32[4,32]{1,0:T(4,128)} %param.26) | copy-start | bytes 1540
  21.0 6.7 %copy-start.1 = (bf16[128,1024]{1,0:T(8,128)(2,1)S(1)}, bf16[128,1024]{1,0:T(8,128)(2,1)}, u32[]{:S(2)}) copy-start(bf16[128,1024]{1,0:T(8,128)(2,1)} %param.14) | copy-start | bytes 786436
  27.8 1.1 copy-start.2
  28.8 12.2 %copy-start.3 = (bf16[128,1024]{1,0:T(8,128)(2,1)S(1)}, bf16[128,1024]{1,0:T(8,128)(2,1)}, u32[]{:S(2)}) copy-start(bf16[128,1024]{1,0:T(8,128)(2,1)} %param.15) | copy-start | bytes 786436
  30.0 11.1 %copy-start.4 = (f32[1024]{0:T(1024)S(1)}, f32[1024]{0:T(1024)}, u32[]{:S(2)}) copy-start(f32[1024]{0:T(1024)} %param.17) | copy-start | bytes 12292
  30.0 10.9 %all-to-all-start = ((f32[4,128,256]{2,1,0:T(8,128)}), f32[4,128,256]{2,1,0:T(8,128)S(1)}, u32[]{:S(2)}, u32[]{:S(2)}) async-start(f32[4,128,256]{2,1,0:T(8,128)} %bitcast), calls=%async_computation | async-start | bytes 1048576 | tf_op jit(solution)/shard_map/all_to_all | solution.py:49
  89.4 2.4 %copy-start.8 = (bf16[1,512,1024]{2,1,0:T(8,128)(2,1)S(1)}, bf16[1,512,1024]{2,1,0:T(8,128)(2,1)}, u32[]{:S(2)}) copy-start(bf16[1,512,1024]{2,1,0:T(8,128)(2,1)} %param.20) | copy-start | bytes 3145732
  94.4 5.7 %copy-start.6 = (f32[128,8]{0,1:T(8,128)S(1)}, f32[128,8]{0,1:T(8,128)}, u32[]{:S(2)}) copy-start(f32[128,8]{0,1:T(8,128)} %param.27) | copy-start | bytes 12292
  94.4 35.8 %all-to-all-start.2 = ((bf16[128,8,1024]{2,1,0:T(8,128)(2,1)}), bf16[128,8,1024]{2,1,0:T(8,128)(2,1)}, u32[]{:S(2)}, u32[]{:S(2)}) async-start(bf16[128,8,1024]{2,1,0:T(8,128)(2,1)} %convert_bitcast_fusion), calls=%async_computation.2 | async-start | bytes 4194304 | tf_op jit(solution)/shard_map/all_to_all | solution.py:107
  138.2 2.5 %copy-start.5 = (f32[1024]{0:T(1024)S(1)}, f32[1024]{0:T(1024)}, u32[]{:S(2)}) copy-start(f32[1024]{0:T(1024)} %param.18) | copy-start | bytes 12292
